TPU v7x, 32 devices: a whole 2x2x4 slice. The times are simulated.
32 devices in a mesh: groups: 2 (over y), tensor: 4 (over z), dp: 4 (over x, core).
Axes of the slice: x: 2, y: 2, z: 4, core: 2. Of those that a mesh axis runs over, the one named last changes fastest.
Arguments:
- hidden: bfloat16 [4096, 8192], P(('groups', 'dp'), 'tensor'), parts along dimension 0, may hold values from -6 to 6
- output_weight: bfloat16 [8192, 8192], P('tensor'), may hold values from -0.0625 to 0.0625
- adapter_down_maps: bfloat16 [256, 64, 8192], P('dp', None, 'tensor'), may hold values from -0.0625 to 0.0625
- adapter_up_maps: bfloat16 [256, 64, 8192], P('dp', None, 'tensor'), may hold values from -0.75 to 0.75
- adapter_slot: int32 [512], P('groups'), parts along dimension 0, may hold values from 0 to 255, as said below
- segment_adapter: int32 [256], P(('groups', 'dp')), parts along dimension 0, may hold values from 0 to 255, as said below
Outputs:
- projected: bfloat16 [4096, 8192], P(('groups', 'dp'), 'tensor'), parts along dimension 0
There are 2 independent parts, one for each index of `groups`. A program takes and returns all parts, laid end to end along the dimension named above; an argument that names none is the same for every part. Nothing has to cross between parts.
Inputs may be any that keep to these rules, and one draw needn't show every extreme that they name: adapter_slot names each of the 256 slots once; slot q is stored on dp index q // 64. `segment_adapter`: among the 32 blocks of one dp index, at most 16 have adapters stored on any one dp index; in every draw one dp index holds the adapters of exactly 16 blocks of every dp index.
All inputs are finite; a program needn't handle non-finite values.
Results may differ from a plain program's by a relative error of at most 0.001.
Values may be sent and summed in bfloat16 or wider, within the bound.
A program may use at most 256 MiB of HBM per device.

v0:
```python
import functools

import jax
import jax.numpy as jnp
from jax import lax
from jax.experimental import pallas as pl
from jax.experimental.pallas import tpu as pltpu
from jax.sharding import PartitionSpec as P

MIB = 1024 * 1024
STEP = 8


def down_kernel(step, slots_ref, rows_ref, *refs):
    maps, out_ref = refs[:step], refs[step]
    for i in range(step):
        out_ref[i] = lax.dot_general(
            rows_ref[i], maps[i][0], (((1,), (1,)), ((), ())),
            preferred_element_type=jnp.float32,
        )


def up_kernel(step, slots_ref, rank_ref, *refs):
    maps, out_ref = refs[:step], refs[step]
    for i in range(step):
        rank = rank_ref[i]
        block = rank.shape[0]
        high = rank.astype(jnp.bfloat16)
        rest = rank - high.astype(jnp.float32)
        mid = rest.astype(jnp.bfloat16)
        low = (rest - mid.astype(jnp.float32)).astype(jnp.bfloat16)
        parts = jnp.concatenate([high, mid, low], axis=0)
        got = jnp.dot(parts, maps[i][0], preferred_element_type=jnp.float32)
        out_ref[i] = (got[2 * block:] + got[block:2 * block]) + got[:block]


def map_specs(step, maps):
    shape = (1,) + maps.shape[1:]

    def spec(i):
        return pl.BlockSpec(shape, lambda g, slots: (slots[g * step + i], 0, 0))

    return [spec(i) for i in range(step)]


def apply_maps(kernel, slots, values, maps, out_tail):
    count = slots.shape[0]
    step = STEP if count % STEP == 0 else 1
    tail = values.shape[1:]
    return pl.pallas_call(
        functools.partial(kernel, step),
        grid_spec=pltpu.PrefetchScalarGridSpec(
            num_scalar_prefetch=1,
            grid=(count // step,),
            in_specs=[pl.BlockSpec((step,) + tail, lambda g, slots: (g, 0, 0))]
            + map_specs(step, maps),
            out_specs=pl.BlockSpec((step,) + out_tail, lambda g, slots: (g, 0, 0)),
        ),
        out_shape=jax.ShapeDtypeStruct((count,) + out_tail, jnp.float32),
        compiler_params=pltpu.CompilerParams(vmem_limit_bytes=40 * MIB),
    )(slots, values, *([maps] * step))


def shift(x, by, count):
    return lax.ppermute(x, "dp", [(i, (i + by) % count) for i in range(count)])


def per_device(
    hidden, output_weight, adapter_down_maps, adapter_up_maps, adapter_slot, segment_adapter
):
    rows, width = hidden.shape
    segs = segment_adapter.shape[0]
    block = rows // segs
    stored, rank_dim, _ = adapter_down_maps.shape
    dp = lax.axis_size("dp")
    me = lax.axis_index("dp")
    cap = segs // 2
    slot = adapter_slot[segment_adapter]
    rel = (slot // stored - me) % dp
    local = slot % stored
    mask = rel[None, :] == jnp.arange(dp, dtype=jnp.int32)[:, None]
    running = jnp.cumsum(mask.astype(jnp.int32), axis=1) - 1
    position = jnp.sum(jnp.where(mask, running, 0), axis=0)
    match = mask[:, None, :] & (
        position[None, None, :] == jnp.arange(cap, dtype=jnp.int32)[None, :, None]
    )
    picked = jnp.sum(
        jnp.where(match, jnp.arange(segs, dtype=jnp.int32)[None, None, :], 0), axis=2
    )
    wanted = jnp.sum(jnp.where(match, local[None, None, :], 0), axis=2)
    place = rel * cap + position
    seg_rows = hidden.reshape(segs, block, width)
    out_rows = seg_rows[picked]
    got_slots = [wanted[0]] + [shift(wanted[k], k, dp) for k in range(1, dp)]
    got_rows = [out_rows[0]] + [shift(out_rows[k], k, dp) for k in range(1, dp)]
    slots = jnp.concatenate(got_slots)
    there_rows = jnp.concatenate(got_rows)
    rank = apply_maps(down_kernel, slots, there_rows, adapter_down_maps, (block, rank_dim))
    rank = lax.psum(rank, "tensor")
    delta = apply_maps(up_kernel, slots, rank, adapter_up_maps, (block, width))
    delta = delta.reshape(dp, cap, block, width)
    back = [delta[0]] + [shift(delta[k], dp - k, dp) for k in range(1, dp)]
    delta_rows = jnp.concatenate(back)[place].reshape(rows, width)
    base = lax.psum_scatter(
        lax.dot_general(
            output_weight, hidden, (((0,), (1,)), ((), ())), preferred_element_type=jnp.float32
        ),
        "tensor",
        scatter_dimension=0,
        tiled=True,
    ).T
    return (base + delta_rows).astype(jnp.bfloat16)


def solution(mesh):
    return jax.shard_map(
        per_device,
        mesh=mesh,
        in_specs=(
            P(("groups", "dp"), "tensor"),
            P("tensor", None),
            P("dp", None, "tensor"),
            P("dp", None, "tensor"),
            P("groups"),
            P(("groups", "dp")),
        ),
        out_specs=P(("groups", "dp"), "tensor"),
        check_vma=False,
    )
```

profile of v0, /device:TPU:16, one launch (start us, length us, event | category | flops | bytes accessed | tf_op | source)
XLA Modules:
  0.0 415.2 jit_solution(6766336662850892600)
XLA Ops:
  6.5 0.0 copy-start
  6.5 0.0 all-reduce.2.cloned.1.call-start
  6.5 0.8 compare_select_fusion.2
  7.4 1.4 gather_fusion
  8.8 0.2 reduce_window_sum.11
  9.0 0.2 fusion.2
  9.3 0.1 reshape.228
  9.3 0.0 copy-done
  9.4 2.8 gather_fusion.1
  12.1 2.7 fusion.10
  14.9 1.6 collective-permute-start.4
  16.4 0.0 collective-permute-start.3
  16.4 1.7 collective-permute-start.5
  18.2 0.0 collective-permute-start.2
  18.2 0.5 collective-permute-start.1
  18.7 42.6 %collective-permute-done.2 = s32[16]{0:T(128)S(1)} collective-permute-done((s32[16]{0:T(128)S(1)}, s32[16]{0:T(128)S(1)}, u32[]{:S(2)}, u32[]{:S(2)}) %collective-permute-start.2) | collective-permute-done | bytes 96 | tf_op jit(solution)/shard_map/ppermute | solution.py:65
  61.4 0.8 collective-permute-start
  62.2 0.1 collective-permute-done.1
  62.3 2.2 collective-permute-done
  64.5 0.1 pad_add_fusion.slots_ref
  64.6 0.0 collective-permute-done.4
  64.6 0.0 collective-permute-done.3
  64.6 0.0 collective-permute-done.5
  64.6 0.6 pad_maximum_fusion.1.rows_ref
  65.2 11.3 %shard_map.64 = f32[64,16,64]{2,1,0:T(8,128)} custom-call(s32[64]{0:T(128)S(1)} %pad_add_fusion.slots_ref, bf16[64,16,2048]{2,1,0:T(8,128)(2,1)S(1)} %pad_maximum_fusion.1.rows_ref, bf16[64,64,2048]{2,1,0:T(8,128)(2,1)} %refs_7_.2, bf16[64,64,2048]{2,1,0:T(8,128)(2,1)} %refs_7_.2, bf16[64,64,2048]{2,1,0:T(8,128)(2,1)} %refs_7_.2, ...), custom_call_target="tpu_custom_call" | custom-call | tf_op jit(solution)/shard_map/pallas_call | solution.py:50
  76.5 0.0 all-reduce.2.cloned.1.call-update
  76.6 0.2 reduce-scatter.2.cloned.1.call-start
  76.8 27.0 %fusion.11 = f32[8192,512]{1,0:T(8,128)} fusion(bf16[2048,8192]{1,0:T(8,128)(2,1)} %param.7, bf16[512,2048]{1,0:T(8,128)(2,1)S(1)} %copy-done), kind=kOutput, calls=%fused_computation.49 | convolution fusion | flops 17179869184 | bytes 52428800 | tf_op jit(solution)/shard_map/dot_general | solution.py:105
  103.8 0.0 reduce-scatter.2.cloned.1.call-update
  103.8 11.3 %all-reduce.2.cloned.1.call-done.rank_ref = f32[64,16,64]{2,1,0:T(8,128)} async-done(((f32[64,16,64]{2,1,0:T(8,128)}), f32[64,16,64]{2,1,0:T(8,128)}) %all-reduce.2.cloned.1.call-update) | async-done | bytes 262160 | tf_op jit(solution)/shard_map/psum | solution.py:99
  115.1 0.0 copy-start.2
  115.1 1.0 copy-done.2
  116.1 11.3 %shard_map.65 = f32[64,16,2048]{2,1,0:T(8,128)S(1)} custom-call(s32[64]{0:T(128)S(1)} %pad_add_fusion.slots_ref, f32[64,16,64]{2,1,0:T(8,128)S(1)} %copy-done.2, bf16[64,64,2048]{2,1,0:T(8,128)(2,1)} %refs_7_.3, bf16[64,64,2048]{2,1,0:T(8,128)(2,1)} %refs_7_.3, bf16[64,64,2048]{2,1,0:T(8,128)(2,1)} %refs_7_.3, bf16[64,64,2048]{2,1,0:T(8,128)(2,1)} %refs_7_.3, ...), custom_call_target="tpu_custom_call" | custom-call | tf_op jit(solution)/shard_map/pallas_call | solution.py:50
  127.4 1.0 fusion.9
  128.4 0.1 collective-permute-start.8
  128.5 1.7 collective-permute-start.7
  130.1 1.4 collective-permute-start.6
  131.6 44.2 %collective-permute-done.8 = f32[16,16,2048]{2,1,0:T(8,128)S(1)} collective-permute-done((f32[16,16,2048]{2,1,0:T(8,128)S(1)}, f32[16,16,2048]{2,1,0:T(8,128)S(1)}, u32[]{:S(2)}, u32[]{:S(2)}) %collective-permute-start.8) | collective-permute-done | bytes 2097184 | tf_op jit(solution)/shard_map/ppermute | solution.py:65
  175.8 1.2 collective-permute-done.7
  177.0 43.5 %collective-permute-done.6 = f32[16,16,2048]{2,1,0:T(8,128)S(1)} collective-permute-done((f32[16,16,2048]{2,1,0:T(8,128)S(1)}, f32[16,16,2048]{2,1,0:T(8,128)S(1)}, u32[]{:S(2)}, u32[]{:S(2)}) %collective-permute-start.6) | collective-permute-done | bytes 2097184 | tf_op jit(solution)/shard_map/ppermute | solution.py:65
  220.5 3.8 pad_maximum_fusion
  224.2 6.2 %gather_fusion.2 = f32[32,16,2048]{2,1,0:T(8,128)} fusion(f32[64,16,2048]{2,1,0:T(8,128)} %pad_maximum_fusion, s32[1024]{0:T(1024)S(1)} %pad_clamp_fusion), kind=kCustom, calls=%fused_computation.2 | custom fusion | bytes 8388736 | tf_op jit(solution)/shard_map/gather | solution.py:103
  230.4 5.4 %copy.11 = f32[512,2048]{0,1:T(8,128)} copy(f32[512,2048]{1,0:T(8,128)} %bitcast.39) | data formatting | bytes 8388608 | tf_op jit(solution)/shard_map/reshape | solution.py:103
  235.8 163.0 %reduce-scatter.2.cloned.1.call-done = f32[2048,512]{1,0:T(8,128)} async-done(((f32[8192,512]{1,0:T(8,128)}), f32[2048,512]{1,0:T(8,128)}) %reduce-scatter.2.cloned.1.call-update) | async-done | bytes 4194320 | tf_op jit(solution)/shard_map/reduce_scatter | solution.py:104
  398.8 0.0 copy-start.1
  398.8 5.6 %fusion = bf16[512,2048]{0,1:T(8,128)(2,1)} fusion(f32[512,2048]{0,1:T(8,128)} %copy.11, f32[2048,512]{1,0:T(8,128)} %reduce-scatter.2.cloned.1.call-done), kind=kLoop, calls=%fused_computation.6 | loop fusion | flops 2097152 | bytes 10485760 | tf_op jit(solution)/shard_map/convert_element_type | solution.py:112
  404.5 3.9 copy.12
  408.4 0.0 copy-done.1
  (10 shorter events, 0.1 us)
Async XLA Ops:
  6.5 2.8 copy-start
  6.5 108.5 %all-reduce.2.cloned.1.call-start = ((), (), s32[]{:S(2)}) async-start(), calls=%async_computation.2 | async-start | bytes 1048576 | tf_op jit(solution)/shard_map/psum | solution.py:99
  14.9 49.7 %collective-permute-start.4 = (bf16[16,16,2048]{2,1,0:T(8,128)(2,1)S(1)}, bf16[16,16,2048]{2,1,0:T(8,128)(2,1)S(1)}, u32[]{:S(2)}, u32[]{:S(2)}) collective-permute-start(bf16[16,16,2048]{2,1,0:T(8,128)(2,1)S(1)} %get-tuple-element.12), channel_id=1, source_target_pairs={{0,2},{1,3},{2,0},{3,1},{4,6},{5,7},{6,4},{7,5},{8,10},{9,11},{10,... | collective-permute-start | bytes 3145736 | tf_op jit(solution)/shard_map/ppermute | solution.py:65
  16.4 48.2 %collective-permute-start.3 = (bf16[16,16,2048]{2,1,0:T(8,128)(2,1)S(1)}, bf16[16,16,2048]{2,1,0:T(8,128)(2,1)S(1)}, u32[]{:S(2)}, u32[]{:S(2)}) collective-permute-start(bf16[16,16,2048]{2,1,0:T(8,128)(2,1)S(1)} %get-tuple-element.13), channel_id=1, source_target_pairs={{0,1},{1,2},{2,3},{3,0},{4,5},{5,6},{6,7},{7,4},{8,9},{9,10},{10,1... | collective-permute-start | bytes 3145736 | tf_op jit(solution)/shard_map/ppermute | solution.py:65
  16.4 48.2 %collective-permute-start.5 = (bf16[16,16,2048]{2,1,0:T(8,128)(2,1)S(1)}, bf16[16,16,2048]{2,1,0:T(8,128)(2,1)S(1)}, u32[]{:S(2)}, u32[]{:S(2)}) collective-permute-start(bf16[16,16,2048]{2,1,0:T(8,128)(2,1)S(1)} %get-tuple-element.14), channel_id=1, source_target_pairs={{0,3},{1,0},{2,1},{3,2},{4,7},{5,4},{6,5},{7,6},{8,11},{9,8},{10,9... | collective-permute-start | bytes 3145736 | tf_op jit(solution)/shard_map/ppermute | solution.py:65
  18.2 43.2 %collective-permute-start.2 = (s32[16]{0:T(128)S(1)}, s32[16]{0:T(128)S(1)}, u32[]{:S(2)}, u32[]{:S(2)}) collective-permute-start(s32[16]{0:T(128)S(1)} %get-tuple-element.16), channel_id=1, source_target_pairs={{0,3},{1,0},{2,1},{3,2},{4,7},{5,4},{6,5},{7,6},{8,11},{9,8},{10,9... | collective-permute-start | bytes 200 | tf_op jit(solution)/shard_map/ppermute | solution.py:65
  18.2 44.1 %collective-permute-start.1 = (s32[16]{0:T(128)S(1)}, s32[16]{0:T(128)S(1)}, u32[]{:S(2)}, u32[]{:S(2)}) collective-permute-start(s32[16]{0:T(128)S(1)} %get-tuple-element.17), channel_id=1, source_target_pairs={{0,2},{1,3},{2,0},{3,1},{4,6},{5,7},{6,4},{7,5},{8,10},{9,11},{10,... | collective-permute-start | bytes 200 | tf_op jit(solution)/shard_map/ppermute | solution.py:65
  61.4 3.2 collective-permute-start
  76.6 322.3 %reduce-scatter.2.cloned.1.call-start = ((), (), s32[]{:S(2)}) async-start(), calls=%async_computation.1 | async-start | bytes 20971520 | tf_op jit(solution)/shard_map/reduce_scatter | solution.py:104
  115.1 1.0 copy-start.2
  128.4 47.4 %collective-permute-start.8 = (f32[16,16,2048]{2,1,0:T(8,128)S(1)}, f32[16,16,2048]{2,1,0:T(8,128)S(1)}, u32[]{:S(2)}, u32[]{:S(2)}) collective-permute-start(f32[16,16,2048]{2,1,0:T(8,128)S(1)} %get-tuple-element.8), channel_id=1, source_target_pairs={{0,1},{1,2},{2,3},{3,0},{4,5},{5,6},{6,7},{7,4},{8,9},{9,10},{10,1... | collective-permute-start | bytes 6291464 | tf_op jit(solution)/shard_map/ppermute | solution.py:65
  128.5 48.5 %collective-permute-start.7 = (f32[16,16,2048]{2,1,0:T(8,128)S(1)}, f32[16,16,2048]{2,1,0:T(8,128)S(1)}, u32[]{:S(2)}, u32[]{:S(2)}) collective-permute-start(f32[16,16,2048]{2,1,0:T(8,128)S(1)} %get-tuple-element.9), channel_id=1, source_target_pairs={{0,2},{1,3},{2,0},{3,1},{4,6},{5,7},{6,4},{7,5},{8,10},{9,11},{10,... | collective-permute-start | bytes 6291464 | tf_op jit(solution)/shard_map/ppermute | solution.py:65
  130.1 90.3 %collective-permute-start.6 = (f32[16,16,2048]{2,1,0:T(8,128)S(1)}, f32[16,16,2048]{2,1,0:T(8,128)S(1)}, u32[]{:S(2)}, u32[]{:S(2)}) collective-permute-start(f32[16,16,2048]{2,1,0:T(8,128)S(1)} %get-tuple-element.10), channel_id=1, source_target_pairs={{0,3},{1,0},{2,1},{3,2},{4,7},{5,4},{6,5},{7,6},{8,11},{9,8},{10,9... | collective-permute-start | bytes 6291464 | tf_op jit(solution)/shard_map/ppermute | solution.py:65
  398.8 9.6 %copy-start.1 = (bf16[512,2048]{1,0:T(8,128)(2,1)S(1)}, bf16[512,2048]{1,0:T(8,128)(2,1)}, u32[]{:S(2)}) copy-start(bf16[512,2048]{1,0:T(8,128)(2,1)} %param.6) | copy-start | bytes 6291460
Sparse Core Ops, SparseCore 0:
  76.7 38.3 all-reduce.1
  117.4 281.3 reduce-scatter.1
where the time goes:
time: 417 us; the launch traced here: 415 us
  waiting for transfers between devices  308 us (74%)
  matrix products  27 us (6%)
  local copies, waits for them, and re-layouts  24.5 us (6%)
  Pallas kernels  22.7 us (5%)
  between operations  13.5 us (3%)
  other arithmetic  11.4 us (3%)
  starting transfers between devices  8.04 us (2%)
    reduce_scatter x1, waiting for transfers between devices, per_device(): lax.psum_scatter(lax.dot_general(output_weight, hidden, (((0,), (1,)), ((...  163 us
    ppermute x9, waiting for transfers between devices, shift(): return lax.ppermute(x, 'dp', [(i, (i + by) % count) for i in range(count)])  134 us
    dot_general x1, matrix products, per_device(): lax.dot_general(output_weight, hidden, (((0,), (1,)), ((), ())), preferre...  27 us
    pallas_call x2, Pallas kernels, apply_maps(): pl.pallas_call(functools.partial(kernel, step), grid_spec=pltpu.PrefetchS...  22.7 us
    psum x1, waiting for transfers between devices, per_device(): rank = lax.psum(rank, 'tensor')  11.3 us
  transfers between devices with their start and end apart: 11, of which 8 were waited for; matrix products, arithmetic and copies ran while one was open for 10% of the time, Pallas kernels for 3%

commit v1 on v0

--- a/solution.py
+++ b/solution.py
@@ -59,6 +59,390 @@
         out_shape=jax.ShapeDtypeStruct((count,) + out_tail, jnp.float32),
         compiler_params=pltpu.CompilerParams(vmem_limit_bytes=40 * MIB),
     )(slots, values, *([maps] * step))
+
+
+FINE = 128.0
+TOP = 32767.0
+MESH = pl.DeviceIdType.MESH
+
+
+def pack(ref, at, value):
+    rows, cols = value.shape
+    top = jnp.maximum(jnp.max(jnp.abs(value), axis=0, keepdims=True), 1e-30)
+    code = jnp.ceil(jnp.log2(top) * FINE + 0.125)
+    scale = jnp.exp2(code * (1.0 / FINE))
+    whole = jnp.round(jnp.clip(value * (TOP / scale), -TOP, TOP))
+    ref[at, :rows, :] = whole.astype(jnp.int32).astype(jnp.int16)
+    ref[at, rows:, :] = jnp.broadcast_to(code.astype(jnp.int32), (16, cols)).astype(jnp.int16)
+
+
+def unpack(ref, at, rows):
+    code = ref[at, rows:, :].astype(jnp.int32).astype(jnp.float32)[:1]
+    scale = jnp.exp2(code * (1.0 / FINE)) * (1.0 / TOP)
+    return ref[at, :rows, :].astype(jnp.int32).astype(jnp.float32) * scale
+
+
+def greet(axis, me, last):
+    barrier = pltpu.get_barrier_semaphore()
+
+    @pl.when(me > 0)
+    def _():
+        pl.semaphore_signal(barrier, inc=1, device_id={axis: me - 1}, device_id_type=MESH)
+
+    @pl.when(me < last)
+    def _():
+        pl.semaphore_signal(barrier, inc=1, device_id={axis: me + 1}, device_id_type=MESH)
+
+    ends = jnp.logical_or(me == 0, me == last)
+
+    @pl.when(ends)
+    def _():
+        pl.semaphore_wait(barrier, 1)
+
+    @pl.when(jnp.logical_not(ends))
+    def _():
+        pl.semaphore_wait(barrier, 2)
+
+
+def first_kernel(
+    axis, count, pieces, hidden_ref, weight_ref, out_ref, weights, send, weight_sem, send_sem,
+    recv_sem,
+):
+    me = lax.axis_index(axis)
+    cols = weights.shape[2]
+    last = count - 1
+
+    def weight_copy(number, c):
+        return pltpu.make_async_copy(
+            weight_ref.at[:, pl.ds(pl.multiple_of(number * cols, cols), cols)],
+            weights.at[c],
+            weight_sem.at[c],
+        )
+
+    def copy(side, c, to):
+        return pltpu.make_async_remote_copy(
+            src_ref=send.at[c],
+            dst_ref=out_ref.at[side, c],
+            send_sem=send_sem.at[c],
+            recv_sem=recv_sem.at[side, c],
+            device_id={axis: to},
+            device_id_type=MESH,
+        )
+
+    ends = jnp.logical_or(me == 0, me == last)
+
+    @pl.when(ends)
+    def _():
+        pl.semaphore_wait(barrier, 1)
+
+    @pl.when(jnp.logical_not(ends))
+    def _():
+        pl.semaphore_wait(barrier, 2)
+
+
+def first_kernel(
+    axis, count, pieces, hidden_ref, weight_ref, out_ref, weights, send, weight_sem, send_sem,
+    recv_sem,
+):
+    me = lax.axis_index(axis)
+    cols = weights.shape[2]
+    last = count - 1
+
+    def weight_copy(number, c):
+        return pltpu.make_async_copy(
+            weight_ref.at[:, pl.ds(pl.multiple_of(number * cols, cols), cols)],
+            weights.at[c],
+            weight_sem.at[c],
+        )
+
+    def copy(side, c, to):
+        return pltpu.make_async_remote_copy(
+            src_ref=send.at[c],
+            dst_ref=out_ref.at[side, c],
+            send_sem=send_sem.at[c],
+            recv_sem=recv_sem.at[side, c],
+            device_id={axis: to},
+            device_id_type=MESH,
+        )
+
+    def run(side, chunk, to):
+        for c in range(pieces):
+            weight_copy(chunk * pieces + c, c).start()
+        greet(axis, me, last)
+
+        def piece(c, carry):
+            weight_copy(chunk * pieces + c, c).wait()
+            pack(
+                send, c,
+                jnp.dot(hidden_ref[...], weights[c], preferred_element_type=jnp.float32),
+            )
+            copy(side, c, to).start()
+            return carry
+
+        lax.fori_loop(0, pieces, piece, 0)
+        for c in range(pieces):
+            copy(side, c, to).wait_send()
+
+    ends = jnp.logical_or(me == 0, me == last)
+    side = jnp.where(me == 0, 0, 1)
+    chunk = jnp.where(me == 0, last, 0)
+    to = jnp.where(me == 0, 1, last - 1)
+
+    @pl.when(ends)
+    def _():
+        for c in range(pieces):
+            weight_copy(chunk * pieces + c, c).start()
+
+    greet(axis, me, last)
+
+    @pl.when(ends)
+    def _():
+        def piece(c, carry):
+            weight_copy(chunk * pieces + c, c).wait()
+            value = jnp.dot(hidden_ref[...], weights[c], preferred_element_type=jnp.float32)
+            pack(send, c, value)
+            copy(side, c, to).start()
+            return carry
+
+        lax.fori_loop(0, pieces, piece, 0)
+        for c in range(pieces):
+            copy(side, c, to).wait_send()
+
+    @pl.when(me == 1)
+    def _():
+        for c in range(pieces):
+            copy(0, c, 0).wait_recv()
+
+    @pl.when(me == last - 1)
+    def _():
+        for c in range(pieces):
+            copy(1, c, last).wait_recv()
+
+
+def rest_kernel(
+    axis, count, pieces, hidden_ref, weight_ref, first_ref, out_ref, weights, send, recv,
+    weight_sem, first_sem, send_sem, recv_sem,
+):
+    me = lax.axis_index(axis)
+    rows = hidden_ref.shape[0]
+    cols = weights.shape[2]
+    last = count - 1
+    total = count * pieces
+
+    def weight_copy(number):
+        return pltpu.make_async_copy(
+            weight_ref.at[:, pl.ds(pl.multiple_of(number * cols, cols), cols)],
+            weights.at[number],
+            weight_sem.at[number],
+        )
+
+    def first_copy(side, c):
+        number = c if side else last * pieces + c
+        return pltpu.make_async_copy(
+            first_ref.at[side, c], recv.at[number], first_sem.at[side, c]
+        )
+
+    @pl.when(me == 1)
+    def _():
+        for c in range(pieces):
+            first_copy(0, c).start()
+
+    @pl.when(me == last - 1)
+    def _():
+        for c in range(pieces):
+            first_copy(1, c).start()
+
+    skip = jnp.where(jnp.logical_or(me == 0, me == last), pieces, 0)
+
+    def fetch(i, carry):
+        @pl.when(2 * me < count)
+        def _():
+            weight_copy(total - 1 - i).start()
+
+        @pl.when(2 * me >= count)
+        def _():
+            weight_copy(i).start()
+
+        return carry
+
+    lax.fori_loop(skip, total, fetch, 0)
+    greet(axis, me, last)
+
+    def own(number):
+        weight_copy(number).wait()
+        return jnp.dot(hidden_ref[...], weights[number], preferred_element_type=jnp.float32)
+
+    def copy(side, number, slot, c, to):
+        return pltpu.make_async_remote_copy(
+            src_ref=send.at[side * pieces + c],
+            dst_ref=recv.at[slot],
+            send_sem=send_sem.at[side, number],
+            recv_sem=recv_sem.at[side, number],
+            device_id={axis: to},
+            device_id_type=MESH,
+        )
+
+    right = jnp.where(me == last, last - 1, me + 1)
+    left = jnp.where(me == 0, 1, me - 1)
+
+    def stage(step, carry):
+        def piece(c, carry):
+            number = (last - step + me) * pieces + c
+
+            @pl.when(step >= me)
+            def _():
+                value = own(number)
+
+                @pl.when(step > jnp.where(me == 0, 1, me))
+                def _():
+                    copy(0, number + pieces, number + pieces, c, right).wait_send()
+
+                @pl.when(me == 0)
+                def _():
+                    pack(send, c, value)
+
+                @pl.when(me > 0)
+                def _():
+                    @pl.when(jnp.logical_and(me == 1, step == 1))
+                    def _():
+                        pltpu.make_async_copy(
+                            first_ref.at[0, c], recv.at[last * pieces + c], first_sem.at[0, c]
+                        ).wait()
+
+                    @pl.when(jnp.logical_not(jnp.logical_and(me == 1, step == 1)))
+                    def _():
+                        copy(0, number, number, c, right).wait_recv()
+
+                    pack(send, c, value + unpack(recv, number, rows))
+
+                copy(0, number, number, c, right).start()
+
+            other = (step - last + me) * pieces + c
+
+            @pl.when(step >= last - me)
+            def _():
+                value = own(other)
+
+                @pl.when(step > jnp.where(me == last, 1, last - me))
+                def _():
+                    copy(1, other - pieces, other - pieces, c, left).wait_send()
+
+                @pl.when(me == last)
+                def _():
+                    pack(send, pieces + c, value)
+
+                @pl.when(me < last)
+                def _():
+                    @pl.when(jnp.logical_and(me == last - 1, step == 1))
+                    def _():
+                        pltpu.make_async_copy(
+                            first_ref.at[1, c], recv.at[c], first_sem.at[1, c]
+                        ).wait()
+
+                    @pl.when(jnp.logical_not(jnp.logical_and(me == last - 1, step == 1)))
+                    def _():
+                        copy(1, other, other, c, left).wait_recv()
+
+                    pack(send, pieces + c, value + unpack(recv, other, rows))
+
+                slot = jnp.where(step == last - 1, total + c, other)
+                copy(1, other, slot, c, left).start()
+
+            return carry
+
+        return lax.fori_loop(0, pieces, piece, carry)
+
+    lax.fori_loop(1, last, stage, 0)
+
+    def finish(c, carry):
+        number = me * pieces + c
+        out_ref[c] = own(number)
+
+        @pl.when(me > 0)
+        def _():
+            copy(0, number, number, c, right).wait_recv()
+            out_ref[c] = out_ref[c] + unpack(recv, number, rows)
+
+        @pl.when(me < last)
+        def _():
+            copy(1, number, total + c, c, left).wait_recv()
+            out_ref[c] = out_ref[c] + unpack(recv, total + c, rows)
+
+        return carry
+
+    lax.fori_loop(0, pieces, finish, 0)
+
+    @pl.when(me < last)
+    def _():
+        for c in range(pieces):
+            number = (me + 1) * pieces + c
+            copy(0, number, number, c, right).wait_send()
+
+    @pl.when(me > 0)
+    def _():
+        for c in range(pieces):
+            number = (me - 1) * pieces + c
+            copy(1, number, number, c, left).wait_send()
+
+
+def base_parts(hidden, weight):
+    rows, depth = hidden.shape
+    count = lax.axis_size("tensor")
+    width = weight.shape[1] // count
+    pieces = max(1, width // 512)
+    cols = width // pieces
+    total = count * pieces
+    vmem, hbm = pl.BlockSpec(memory_space=pltpu.VMEM), pl.BlockSpec(memory_space=pl.ANY)
+    dma = pltpu.SemaphoreType.DMA
+
+    def packed(number):
+        return pltpu.VMEM((number, rows + 16, cols), jnp.int16)
+
+    def params(number):
+        return pltpu.CompilerParams(
+            collective_id=number, has_side_effects=True, vmem_limit_bytes=58 * MIB
+        )
+
+    def cost(us):
+        return pl.CostEstimate(flops=us * 1000000000, bytes_accessed=us * 1000000, transcendentals=0)
+
+    def first():
+        return pl.pallas_call(
+            functools.partial(first_kernel, "tensor", count, pieces),
+            out_shape=jax.ShapeDtypeStruct((2, pieces, rows + 16, cols), jnp.int16),
+            in_specs=[vmem, hbm],
+            out_specs=hbm,
+            scratch_shapes=[
+                pltpu.VMEM((pieces, depth, cols), jnp.bfloat16),
+                packed(pieces),
+                dma((pieces,)),
+                dma((pieces,)),
+                dma((2, pieces)),
+            ],
+            compiler_params=params(0),
+            cost_estimate=cost(45),
+        )(hidden, weight)
+
+    def rest(got):
+        return pl.pallas_call(
+            functools.partial(rest_kernel, "tensor", count, pieces),
+            out_shape=jax.ShapeDtypeStruct((pieces, rows, cols), jnp.float32),
+            in_specs=[vmem, hbm, hbm],
+            out_specs=vmem,
+            scratch_shapes=[
+                pltpu.VMEM((total, depth, cols), jnp.bfloat16),
+                packed(2 * pieces),
+                packed(total + pieces),
+                dma((total,)),
+                dma((2, pieces)),
+                dma((2, total)),
+                dma((2, total)),
+            ],
+            compiler_params=params(1),
+            cost_estimate=cost(90),
+        )(hidden, weight, got)
+
+    return first, rest
 
 
 def shift(x, by, count):
@@ -95,20 +479,16 @@
     got_rows = [out_rows[0]] + [shift(out_rows[k], k, dp) for k in range(1, dp)]
     slots = jnp.concatenate(got_slots)
     there_rows = jnp.concatenate(got_rows)
+    first, rest = base_parts(hidden, output_weight)
+    part, there_rows = lax.optimization_barrier((first(), there_rows))
     rank = apply_maps(down_kernel, slots, there_rows, adapter_down_maps, (block, rank_dim))
     rank = lax.psum(rank, "tensor")
     delta = apply_maps(up_kernel, slots, rank, adapter_up_maps, (block, width))
+    part, delta = lax.optimization_barrier((part, delta))
     delta = delta.reshape(dp, cap, block, width)
     back = [delta[0]] + [shift(delta[k], dp - k, dp) for k in range(1, dp)]
     delta_rows = jnp.concatenate(back)[place].reshape(rows, width)
-    base = lax.psum_scatter(
-        lax.dot_general(
-            output_weight, hidden, (((0,), (1,)), ((), ())), preferred_element_type=jnp.float32
-        ),
-        "tensor",
-        scatter_dimension=0,
-        tiled=True,
-    ).T
+    base = rest(part).transpose(1, 0, 2).reshape(rows, width)
     return (base + delta_rows).astype(jnp.bfloat16)
 
 

time: 417 us -> 288 us (0.69)
  waiting for transfers between devices: 308 us -> 41.6 us
  Pallas kernels: 22.7 us -> 179 us
  matrix products: 27 us -> 0 us
  local copies, waits for them, and re-layouts: 24.5 us -> 31.9 us
    reduce_scatter x1 -> x0, waiting for transfers between devices: 163 us -> none  [per_device(): lax.psum_scatter(lax.dot_general(output_weight, hidden, (((0,), (1,)), ((...]
    pallas_call x0 -> x2, Pallas kernels: none -> 156 us  [the longest x1 104 us: rest(): pl.pallas_call(functools.partial(rest_kernel, 'tensor', count, pieces), o...]
    ppermute x9, waiting for transfers between devices: 134 us -> 2.96 us  [shift(): return lax.ppermute(x, 'dp', [(i, (i + by) % count) for i in range(count)])]
    psum x1, waiting for transfers between devices: 11.3 us -> 38.6 us  [per_device(): rank = lax.psum(rank, 'tensor')]
    dot_general x1 -> x0, matrix products: 27 us -> none  [per_device(): lax.dot_general(output_weight, hidden, (((0,), (1,)), ((), ())), preferre...]
    transpose x0 -> x1, local copies, waits for them, and re-layouts: none -> 5.25 us  [per_device(): base = rest(part).transpose(1, 0, 2).reshape(rows, width)]
  transfers between devices with their start and end apart: 11 -> 10, of which waited for: 8 -> 2; matrix products, arithmetic and copies ran while one was open for 10% -> 5% of each run, Pallas kernels for 3% -> 54%
where the time goes in v1:
time: 288 us; the launch traced here: 287 us
  Pallas kernels  179 us (62%)
  waiting for transfers between devices  41.6 us (14%)
  local copies, waits for them, and re-layouts  31.9 us (11%)
  between operations  13.5 us (5%)
  other arithmetic  12.9 us (4%)
  starting transfers between devices  8.89 us (3%)
    pallas_call x1, Pallas kernels, rest(): pl.pallas_call(functools.partial(rest_kernel, 'tensor', count, pieces), o...  104 us
    pallas_call x1, Pallas kernels, first(): pl.pallas_call(functools.partial(first_kernel, 'tensor', count, pieces),...  52.7 us
    psum x1, waiting for transfers between devices, per_device(): rank = lax.psum(rank, 'tensor')  38.6 us
    pallas_call x2, Pallas kernels, apply_maps(): pl.pallas_call(functools.partial(kernel, step), grid_spec=pltpu.PrefetchS...  22.1 us
    ppermute x9, starting transfers between devices, shift(): return lax.ppermute(x, 'dp', [(i, (i + by) % count) for i in range(count)])  8.89 us
    gather x1, local copies, waits for them, and re-layouts, per_device(): delta_rows = jnp.concatenate(back)[place].reshape(rows, width)  6.17 us
    concatenate x1, other arithmetic, per_device(): delta_rows = jnp.concatenate(back)[place].reshape(rows, width)  5.8 us
  transfers between devices with their start and end apart: 10, of which 2 were waited for; matrix products, arithmetic and copies ran while one was open for 5% of the time, Pallas kernels for 54%

profile of v1, /device:TPU:16, one launch (start us, length us, event | category | flops | bytes accessed | tf_op | source)
XLA Modules:
  0.0 287.4 jit_solution(14819779322731659995)
XLA Ops:
  6.5 0.0 copy-start
  6.5 0.0 all-reduce.2.cloned.1.call-start
  6.5 0.7 compare_select_fusion.2
  7.2 0.0 copy-done
  7.2 0.7 gather_fusion
  8.0 0.2 reduce_window_sum.11
  8.2 0.2 fusion.2
  8.4 1.0 collective-permute-start.5
  9.4 0.6 collective-permute-start.4
  10.1 0.1 reshape.232
  10.2 4.3 %gather_fusion.1 = bf16[64,16,2048]{2,1,0:T(8,128)(2,1)} fusion(bf16[32,16,2048]{2,1,0:T(8,128)(2,1)} %bitcast.38, s32[1024]{0:T(1024)S(1)} %pad_clamp_fusion.1), kind=kCustom, calls=%fused_computation.1 | custom fusion | bytes 8388864 | tf_op jit(solution)/shard_map/gather | solution.py:477
  14.5 3.7 %fusion.10 = (bf16[16,16,2048]{2,1,0:T(8,128)(2,1)S(1)}, bf16[16,16,2048]{2,1,0:T(8,128)(2,1)}, bf16[16,16,2048]{2,1,0:T(8,128)(2,1)S(1)}, bf16[16,16,2048]{2,1,0:T(8,128)(2,1)S(1)}) fusion(bf16[64,16,2048]{2,1,0:T(8,128)(2,1)} %gather_fusion.1), kind=kLoop, calls=%fused_computation.48 | loop fusion | bytes 8388608 | tf_op jit(solution)/shard_map/slice | solution.py:479
  18.2 1.4 collective-permute-start.1
  19.6 0.0 collective-permute-start
  19.6 1.7 collective-permute-start.2
  21.4 52.7 %shard_map.64.first_ref = s16[2,4,528,512]{3,2,1,0:T(8,128)(2,1)} custom-call(bf16[512,2048]{1,0:T(8,128)(2,1)} %hidden_ref.3, bf16[2048,8192]{1,0:T(8,128)(2,1)} %weight_ref.3), custom_call_target="tpu_custom_call" | custom-call | flops 44999999488 | bytes 45000000 | tf_op jit(solution)/shard_map/pallas_call | solution.py:410
  74.1 0.0 collective-permute-done.5
  74.1 0.1 collective-permute-start.3
  74.2 0.0 collective-permute-done.4
  74.2 2.9 %collective-permute-done.3 = s32[16]{0:T(128)S(1)} collective-permute-done((s32[16]{0:T(128)S(1)}, s32[16]{0:T(128)S(1)}, u32[]{:S(2)}, u32[]{:S(2)}) %collective-permute-start.3) | collective-permute-done | bytes 96 | tf_op jit(solution)/shard_map/ppermute | solution.py:449
  77.2 0.1 pad_add_fusion.slots_ref
  77.2 0.0 collective-permute-done.1
  77.2 0.0 collective-permute-done
  77.2 0.0 collective-permute-done.2
  77.2 1.6 pad_maximum_fusion.1.rows_ref
  78.9 11.8 %shard_map.65 = f32[64,16,64]{2,1,0:T(8,128)} custom-call(s32[64]{0:T(128)S(1)} %pad_add_fusion.slots_ref, bf16[64,16,2048]{2,1,0:T(8,128)(2,1)S(1)} %pad_maximum_fusion.1.rows_ref, bf16[64,64,2048]{2,1,0:T(8,128)(2,1)} %refs_7_.2, bf16[64,64,2048]{2,1,0:T(8,128)(2,1)} %refs_7_.2, bf16[64,64,2048]{2,1,0:T(8,128)(2,1)} %refs_7_.2, ...), custom_call_target="tpu_custom_call" | custom-call | tf_op jit(solution)/shard_map/pallas_call | solution.py:50
  90.7 0.0 all-reduce.2.cloned.1.call-update
  90.7 38.6 %all-reduce.2.cloned.1.call-done.rank_ref = f32[64,16,64]{2,1,0:T(8,128)} async-done(((f32[64,16,64]{2,1,0:T(8,128)}), f32[64,16,64]{2,1,0:T(8,128)}) %all-reduce.2.cloned.1.call-update) | async-done | bytes 262160 | tf_op jit(solution)/shard_map/psum | solution.py:485
  129.4 0.0 copy-start.2
  129.4 1.0 copy-done.2
  130.4 10.3 %shard_map.66 = f32[64,16,2048]{2,1,0:T(8,128)S(1)} custom-call(s32[64]{0:T(128)S(1)} %pad_add_fusion.slots_ref, f32[64,16,64]{2,1,0:T(8,128)S(1)} %copy-done.2, bf16[64,64,2048]{2,1,0:T(8,128)(2,1)} %refs_7_.3, bf16[64,64,2048]{2,1,0:T(8,128)(2,1)} %refs_7_.3, bf16[64,64,2048]{2,1,0:T(8,128)(2,1)} %refs_7_.3, bf16[64,64,2048]{2,1,0:T(8,128)(2,1)} %refs_7_.3, ...), custom_call_target="tpu_custom_call" | custom-call | tf_op jit(solution)/shard_map/pallas_call | solution.py:50
  140.7 2.8 fusion.9
  143.6 0.0 collective-permute-start.8
  143.6 2.6 collective-permute-start.7
  146.2 1.4 collective-permute-start.6
  147.7 103.7 %shard_map.67 = f32[4,512,512]{2,1,0:T(8,128)} custom-call(bf16[512,2048]{1,0:T(8,128)(2,1)} %hidden_ref.3, bf16[2048,8192]{1,0:T(8,128)(2,1)} %weight_ref.3, s16[2,4,528,512]{3,2,1,0:T(8,128)(2,1)} %shard_map.64.first_ref), custom_call_target="tpu_custom_call" | custom-call | flops 89999998976 | bytes 90000000 | tf_op jit(solution)/shard_map/pallas_call | solution.py:427
  251.4 5.2 %copy.10 = f32[512,4,512]{0,2,1:T(8,128)} copy(f32[512,4,512]{2,0,1:T(8,128)} %bitcast.39) | data formatting | bytes 8388608 | tf_op jit(solution)/shard_map/transpose | solution.py:491
  256.6 0.0 collective-permute-done.8
  256.6 0.0 collective-permute-done.7
  256.6 0.0 collective-permute-done.6
  256.7 5.8 %pad_maximum_fusion = f32[64,16,2048]{2,1,0:T(8,128)} fusion(f32[16,16,2048]{2,1,0:T(8,128)} %collective-permute-done.8, f32[16,16,2048]{2,1,0:T(8,128)} %collective-permute-done.7, f32[16,16,2048]{2,1,0:T(8,128)} %collective-permute-done.6, f32[16,16,2048]{2,1,0:T(8,128)S(1)} %get-tuple-element.15), kind=kLoop, calls=%fused_computation.3 | loop fusion | flops 6291456 | bytes 16777216 | tf_op jit(solution)/shard_map/concatenate | solution.py:490
  262.5 6.2 %gather_fusion.2 = f32[32,16,2048]{2,1,0:T(8,128)} fusion(f32[64,16,2048]{2,1,0:T(8,128)} %pad_maximum_fusion, s32[1024]{0:T(1024)S(1)} %pad_clamp_fusion), kind=kCustom, calls=%fused_computation.2 | custom fusion | bytes 8388736 | tf_op jit(solution)/shard_map/gather | solution.py:490
  268.6 5.4 %copy.11 = f32[512,2048]{0,1:T(8,128)} copy(f32[512,2048]{1,0:T(8,128)} %bitcast.37) | data formatting | bytes 8388608 | tf_op jit(solution)/shard_map/reshape | solution.py:490
  274.0 0.0 copy-start.1
  274.0 4.2 %fusion = bf16[512,2048]{0,1:T(8,128)(2,1)S(1)} fusion(f32[512,2048]{0,1:T(8,128)} %copy.11, f32[512,4,512]{0,2,1:T(8,128)} %copy.10), kind=kLoop, calls=%fused_computation.6 | loop fusion | flops 2097152 | bytes 10485760 | tf_op jit(solution)/shard_map/convert_element_type | solution.py:492
  278.2 2.4 copy.12
  280.6 0.0 copy-done.1
  (10 shorter events, 0.1 us)
Async XLA Ops:
  6.5 0.7 copy-start
  6.5 122.8 %all-reduce.2.cloned.1.call-start = ((), (), s32[]{:S(2)}) async-start(), calls=%async_computation | async-start | bytes 1048576 | tf_op jit(solution)/shard_map/psum | solution.py:485
  8.4 65.7 %collective-permute-start.5 = (s32[16]{0:T(128)S(1)}, s32[16]{0:T(128)S(1)}, u32[]{:S(2)}, u32[]{:S(2)}) collective-permute-start(s32[16]{0:T(128)S(1)} %get-tuple-element.24), channel_id=1, source_target_pairs={{0,3},{1,0},{2,1},{3,2},{4,7},{5,4},{6,5},{7,6},{8,11},{9,8},{10,9... | collective-permute-start | bytes 200 | tf_op jit(solution)/shard_map/ppermute | solution.py:449
  9.4 64.8 %collective-permute-start.4 = (s32[16]{0:T(128)S(1)}, s32[16]{0:T(128)S(1)}, u32[]{:S(2)}, u32[]{:S(2)}) collective-permute-start(s32[16]{0:T(128)S(1)} %get-tuple-element.25), channel_id=1, source_target_pairs={{0,2},{1,3},{2,0},{3,1},{4,6},{5,7},{6,4},{7,5},{8,10},{9,11},{10,... | collective-permute-start | bytes 200 | tf_op jit(solution)/shard_map/ppermute | solution.py:449
  18.2 59.0 %collective-permute-start.1 = (bf16[16,16,2048]{2,1,0:T(8,128)(2,1)}, bf16[16,16,2048]{2,1,0:T(8,128)(2,1)S(1)}, u32[]{:S(2)}, u32[]{:S(2)}) collective-permute-start(bf16[16,16,2048]{2,1,0:T(8,128)(2,1)} %get-tuple-element.20), channel_id=1, source_target_pairs={{0,2},{1,3},{2,0},{3,1},{4,6},{5,7},{6,4},{7,5},{8,10},{9,11},{10,... | collective-permute-start | bytes 3145736 | tf_op jit(solution)/shard_map/ppermute | solution.py:449
  19.6 57.6 %collective-permute-start = (bf16[16,16,2048]{2,1,0:T(8,128)(2,1)S(1)}, bf16[16,16,2048]{2,1,0:T(8,128)(2,1)S(1)}, u32[]{:S(2)}, u32[]{:S(2)}) collective-permute-start(bf16[16,16,2048]{2,1,0:T(8,128)(2,1)S(1)} %get-tuple-element.21), channel_id=1, source_target_pairs={{0,1},{1,2},{2,3},{3,0},{4,5},{5,6},{6,7},{7,4},{8,9},{9,10},{10,1... | collective-permute-start | bytes 3145736 | tf_op jit(solution)/shard_map/ppermute | solution.py:449
  19.6 57.6 %collective-permute-start.2 = (bf16[16,16,2048]{2,1,0:T(8,128)(2,1)S(1)}, bf16[16,16,2048]{2,1,0:T(8,128)(2,1)}, u32[]{:S(2)}, u32[]{:S(2)}) collective-permute-start(bf16[16,16,2048]{2,1,0:T(8,128)(2,1)S(1)} %get-tuple-element.22), channel_id=1, source_target_pairs={{0,3},{1,0},{2,1},{3,2},{4,7},{5,4},{6,5},{7,6},{8,11},{9,8},{10,9... | collective-permute-start | bytes 3145736 | tf_op jit(solution)/shard_map/ppermute | solution.py:449
  74.1 3.0 %collective-permute-start.3 = (s32[16]{0:T(128)S(1)}, s32[16]{0:T(128)S(1)}, u32[]{:S(2)}, u32[]{:S(2)}) collective-permute-start(s32[16]{0:T(128)S(1)} %get-tuple-element.26), channel_id=1, source_target_pairs={{0,1},{1,2},{2,3},{3,0},{4,5},{5,6},{6,7},{7,4},{8,9},{9,10},{10,1... | collective-permute-start | bytes 200 | tf_op jit(solution)/shard_map/ppermute | solution.py:449
  129.4 1.0 copy-start.2
  143.6 113.1 %collective-permute-start.8 = (f32[16,16,2048]{2,1,0:T(8,128)}, f32[16,16,2048]{2,1,0:T(8,128)}, u32[]{:S(2)}, u32[]{:S(2)}) collective-permute-start(f32[16,16,2048]{2,1,0:T(8,128)} %get-tuple-element.16), channel_id=1, source_target_pairs={{0,1},{1,2},{2,3},{3,0},{4,5},{5,6},{6,7},{7,4},{8,9},{9,10},{10,1... | collective-permute-start | bytes 6291464 | tf_op jit(solution)/shard_map/ppermute | solution.py:449
  143.6 113.1 %collective-permute-start.7 = (f32[16,16,2048]{2,1,0:T(8,128)}, f32[16,16,2048]{2,1,0:T(8,128)}, u32[]{:S(2)}, u32[]{:S(2)}) collective-permute-start(f32[16,16,2048]{2,1,0:T(8,128)} %get-tuple-element.17), channel_id=1, source_target_pairs={{0,2},{1,3},{2,0},{3,1},{4,6},{5,7},{6,4},{7,5},{8,10},{9,11},{10,... | collective-permute-start | bytes 6291464 | tf_op jit(solution)/shard_map/ppermute | solution.py:449
  146.2 110.4 %collective-permute-start.6 = (f32[16,16,2048]{2,1,0:T(8,128)}, f32[16,16,2048]{2,1,0:T(8,128)}, u32[]{:S(2)}, u32[]{:S(2)}) collective-permute-start(f32[16,16,2048]{2,1,0:T(8,128)} %get-tuple-element.18), channel_id=1, source_target_pairs={{0,3},{1,0},{2,1},{3,2},{4,7},{5,4},{6,5},{7,6},{8,11},{9,8},{10,9... | collective-permute-start | bytes 6291464 | tf_op jit(solution)/shard_map/ppermute | solution.py:449
  274.0 6.6 %copy-start.1 = (s32[256]{0:T(256)S(1)}, s32[256]{0:T(256)}, u32[]{:S(2)}) copy-start(s32[256]{0:T(256)} %param.10) | copy-start | bytes 3076
Sparse Core Ops, SparseCore 0:
  90.8 38.4 all-reduce.1

commit v2 on v1

--- a/solution.py
+++ b/solution.py
@@ -13,18 +13,25 @@
 
 def down_kernel(step, slots_ref, rows_ref, *refs):
     maps, out_ref = refs[:step], refs[step]
-    for i in range(step):
-        out_ref[i] = lax.dot_general(
-            rows_ref[i], maps[i][0], (((1,), (1,)), ((), ())),
-            preferred_element_type=jnp.float32,
+    for i in range(0, step, 2):
+        out_ref[i // 2] = jnp.concatenate(
+            [
+                lax.dot_general(
+                    rows_ref[j], maps[j][0], (((1,), (1,)), ((), ())),
+                    preferred_element_type=jnp.float32,
+                )
+                for j in (i, i + 1)
+            ],
+            axis=1,
         )
 
 
 def up_kernel(step, slots_ref, rank_ref, *refs):
     maps, out_ref = refs[:step], refs[step]
     for i in range(step):
-        rank = rank_ref[i]
-        block = rank.shape[0]
+        pair = rank_ref[i // 2]
+        block, half = pair.shape[0], pair.shape[1] // 2
+        rank = pair[:, (i % 2) * half:(i % 2 + 1) * half]
         high = rank.astype(jnp.bfloat16)
         rest = rank - high.astype(jnp.float32)
         mid = rest.astype(jnp.bfloat16)
@@ -43,20 +50,20 @@
     return [spec(i) for i in range(step)]
 
 
-def apply_maps(kernel, slots, values, maps, out_tail):
+def apply_maps(kernel, slots, values, maps, out_tail, fold_in, fold_out):
     count = slots.shape[0]
-    step = STEP if count % STEP == 0 else 1
+    step = STEP if count % STEP == 0 else 2
     tail = values.shape[1:]
     return pl.pallas_call(
         functools.partial(kernel, step),
         grid_spec=pltpu.PrefetchScalarGridSpec(
             num_scalar_prefetch=1,
             grid=(count // step,),
-            in_specs=[pl.BlockSpec((step,) + tail, lambda g, slots: (g, 0, 0))]
+            in_specs=[pl.BlockSpec((step // fold_in,) + tail, lambda g, slots: (g, 0, 0))]
             + map_specs(step, maps),
-            out_specs=pl.BlockSpec((step,) + out_tail, lambda g, slots: (g, 0, 0)),
+            out_specs=pl.BlockSpec((step // fold_out,) + out_tail, lambda g, slots: (g, 0, 0)),
         ),
-        out_shape=jax.ShapeDtypeStruct((count,) + out_tail, jnp.float32),
+        out_shape=jax.ShapeDtypeStruct((count // fold_out,) + out_tail, jnp.float32),
         compiler_params=pltpu.CompilerParams(vmem_limit_bytes=40 * MIB),
     )(slots, values, *([maps] * step))
 
@@ -443,6 +450,110 @@
         )(hidden, weight, got)
 
     return first, rest
+
+
+def sum_kernel(axis, count, in_ref, out_ref, parts, full, send_sem, recv_sem):
+    me = lax.axis_index(axis)
+    size = parts.shape[1]
+
+    def peer(k):
+        return lax.rem(me + k, count)
+
+    barrier = pltpu.get_barrier_semaphore()
+    for k in range(1, count):
+        pl.semaphore_signal(barrier, inc=1, device_id={axis: peer(k)}, device_id_type=MESH)
+    pl.semaphore_wait(barrier, count - 1)
+
+    def scatter(k):
+        return pltpu.make_async_remote_copy(
+            src_ref=in_ref.at[pl.ds(peer(k) * size, size)],
+            dst_ref=parts.at[k],
+            send_sem=send_sem.at[0, k],
+            recv_sem=recv_sem.at[0, k],
+            device_id={axis: peer(k)},
+            device_id_type=MESH,
+        )
+
+    def gather(k):
+        mine = full.at[pl.ds(me * size, size)]
+        return pltpu.make_async_remote_copy(
+            src_ref=mine,
+            dst_ref=mine,
+            send_sem=send_sem.at[1, k],
+            recv_sem=recv_sem.at[1, k],
+            device_id={axis: peer(k)},
+            device_id_type=MESH,
+        )
+
+    for k in range(1, count):
+        scatter(k).start()
+    total = in_ref[pl.ds(me * size, size)]
+    for k in range(1, count):
+        scatter(k).wait_recv()
+        total = total + parts[k]
+    full[pl.ds(me * size, size)] = total
+    for k in range(1, count):
+        gather(k).start()
+    for k in range(1, count):
+        gather(k).wait_recv()
+    out_ref[...] = full[...]
+    for k in range(1, count):
+        scatter(k).wait_send()
+        gather(k).wait_send()
+
+
+def sum_over_tensor(x):
+    count = lax.axis_size("tensor")
+    size = x.shape[0] // count
+    vmem = pl.BlockSpec(memory_space=pltpu.VMEM)
+    return pl.pallas_call(
+        functools.partial(sum_kernel, "tensor", count),
+        out_shape=jax.ShapeDtypeStruct(x.shape, x.dtype),
+        in_specs=[vmem],
+        out_specs=vmem,
+        scratch_shapes=[
+            pltpu.VMEM((count, size) + x.shape[1:], x.dtype),
+            pltpu.VMEM(x.shape, x.dtype),
+            pltpu.SemaphoreType.DMA((2, count)),
+            pltpu.SemaphoreType.DMA((2, count)),
+        ],
+        compiler_params=pltpu.CompilerParams(
+            collective_id=2, has_side_effects=True, vmem_limit_bytes=16 * MIB
+        ),
+    )(x)
+
+
+def join_kernel(held_ref, rel_ref, base_ref, *refs):
+    deltas, out_ref = refs[:-1], refs[-1]
+    pieces, _, cols = base_ref.shape
+    for k, delta in enumerate(deltas):
+        @pl.when(rel_ref[pl.program_id(0)] == k)
+        def _():
+            for c in range(pieces):
+                part = slice(c * cols, (c + 1) * cols)
+                out_ref[:, part] = (base_ref[c] + delta[0, :, part]).astype(out_ref.dtype)
+
+
+def join(base, deltas, held, rel):
+    pieces, rows, cols = base.shape
+    segs = rel.shape[0]
+    _, block, width = deltas[0].shape
+
+    def spec(k):
+        return pl.BlockSpec((1, block, width), lambda s, held, rel: (held[k * segs + s], 0, 0))
+
+    return pl.pallas_call(
+        join_kernel,
+        grid_spec=pltpu.PrefetchScalarGridSpec(
+            num_scalar_prefetch=2,
+            grid=(segs,),
+            in_specs=[pl.BlockSpec((pieces, block, cols), lambda s, held, rel: (0, s, 0))]
+            + [spec(k) for k in range(len(deltas))],
+            out_specs=pl.BlockSpec((block, width), lambda s, held, rel: (s, 0)),
+        ),
+        out_shape=jax.ShapeDtypeStruct((rows, width), jnp.bfloat16),
+        compiler_params=pltpu.CompilerParams(vmem_limit_bytes=16 * MIB),
+    )(held, rel, base, *deltas)
 
 
 def shift(x, by, count):
@@ -472,7 +583,7 @@
         jnp.where(match, jnp.arange(segs, dtype=jnp.int32)[None, None, :], 0), axis=2
     )
     wanted = jnp.sum(jnp.where(match, local[None, None, :], 0), axis=2)
-    place = rel * cap + position
+    held = jnp.clip(running, 0, cap - 1).astype(jnp.int32).reshape(-1)
     seg_rows = hidden.reshape(segs, block, width)
     out_rows = seg_rows[picked]
     got_slots = [wanted[0]] + [shift(wanted[k], k, dp) for k in range(1, dp)]
@@ -481,15 +592,13 @@
     there_rows = jnp.concatenate(got_rows)
     first, rest = base_parts(hidden, output_weight)
     part, there_rows = lax.optimization_barrier((first(), there_rows))
-    rank = apply_maps(down_kernel, slots, there_rows, adapter_down_maps, (block, rank_dim))
-    rank = lax.psum(rank, "tensor")
-    delta = apply_maps(up_kernel, slots, rank, adapter_up_maps, (block, width))
+    rank = apply_maps(down_kernel, slots, there_rows, adapter_down_maps, (block, 2 * rank_dim), 1, 2)
+    rank = sum_over_tensor(rank)
+    delta = apply_maps(up_kernel, slots, rank, adapter_up_maps, (block, width), 2, 1)
     part, delta = lax.optimization_barrier((part, delta))
     delta = delta.reshape(dp, cap, block, width)
     back = [delta[0]] + [shift(delta[k], dp - k, dp) for k in range(1, dp)]
-    delta_rows = jnp.concatenate(back)[place].reshape(rows, width)
-    base = rest(part).transpose(1, 0, 2).reshape(rows, width)
-    return (base + delta_rows).astype(jnp.bfloat16)
+    return join(rest(part), back, held, rel.astype(jnp.int32))
 
 
 def solution(mesh):

time: 288 us -> 241 us (0.84)
  waiting for transfers between devices: 41.6 us -> 2.97 us
  Pallas kernels: 179 us -> 210 us
  local copies, waits for them, and re-layouts: 31.9 us -> 14.2 us
  between operations: 13.5 us -> 0.15 us
  other arithmetic: 12.9 us -> 3.07 us
    psum x1 -> x0, waiting for transfers between devices: 38.6 us -> none  [per_device(): rank = lax.psum(rank, 'tensor')]
    pallas_call x0 -> x2, Pallas kernels: none -> 31.8 us  [the longest x1 17.6 us: join(): pl.pallas_call(join_kernel, grid_spec=pltpu.PrefetchScalarGridSpec(num_sc...]
    gather x1 -> x0, local copies, waits for them, and re-layouts: 6.17 us -> none  [per_device(): delta_rows = jnp.concatenate(back)[place].reshape(rows, width)]
    concatenate x1 -> x0, other arithmetic: 5.8 us -> none  [per_device(): delta_rows = jnp.concatenate(back)[place].reshape(rows, width)]
    reshape x1 -> x0, local copies, waits for them, and re-layouts: 5.37 us -> none  [per_device(): delta_rows = jnp.concatenate(back)[place].reshape(rows, width)]
    transpose x1 -> x0, local copies, waits for them, and re-layouts: 5.25 us -> none  [per_device(): base = rest(part).transpose(1, 0, 2).reshape(rows, width)]
    convert_element_type x1 -> x0, other arithmetic: 4.2 us -> none  [per_device(): return (base + delta_rows).astype(jnp.bfloat16)]
  transfers between devices with their start and end apart: 10 -> 9, of which waited for: 2 -> 1; matrix products, arithmetic and copies ran while one was open for 5% -> 4% of each run, Pallas kernels for 54% -> 66%
where the time goes in v2:
time: 241 us; the launch traced here: 238 us
  Pallas kernels  210 us (87%)
  local copies, waits for them, and re-layouts  14.2 us (6%)
  starting transfers between devices  7.73 us (3%)
  other arithmetic  3.07 us (1%)
  waiting for transfers between devices  2.97 us (1%)
    pallas_call x1, Pallas kernels, rest(): pl.pallas_call(functools.partial(rest_kernel, 'tensor', count, pieces), o...  104 us
    pallas_call x1, Pallas kernels, first(): pl.pallas_call(functools.partial(first_kernel, 'tensor', count, pieces),...  52.7 us
    pallas_call x2, Pallas kernels, apply_maps(): pl.pallas_call(functools.partial(kernel, step), grid_spec=pltpu.PrefetchS...  20.9 us
    pallas_call x1, Pallas kernels, join(): pl.pallas_call(join_kernel, grid_spec=pltpu.PrefetchScalarGridSpec(num_sc...  17.6 us
    pallas_call x1, Pallas kernels, sum_over_tensor(): pl.pallas_call(functools.partial(sum_kernel, 'tensor', count), out_shape=...  14.2 us
    ppermute x9, starting transfers between devices, shift(): return lax.ppermute(x, 'dp', [(i, (i + by) % count) for i in range(count)])  7.73 us
  transfers between devices with their start and end apart: 9, of which 1 were waited for; matrix products, arithmetic and copies ran while one was open for 4% of the time, Pallas kernels for 66%

profile of v2, /device:TPU:16, one launch (start us, length us, event | category | flops | bytes accessed | tf_op | source)
XLA Modules:
  0.0 237.6 jit_solution(13519485328095757322)
XLA Ops:
  0.0 0.0 copy-start
  0.0 0.7 compare_select_fusion.1
  0.7 0.0 copy-done
  0.7 0.7 gather_fusion
  1.4 0.0 copy-start.3
  1.4 0.2 reduce_window_sum.11
  1.7 0.2 fusion.1
  1.9 1.0 collective-permute-start.5
  2.9 0.6 collective-permute-start.4
  3.6 0.1 reshape.127
  3.6 4.4 %gather_fusion.1 = bf16[64,16,2048]{2,1,0:T(8,128)(2,1)} fusion(bf16[32,16,2048]{2,1,0:T(8,128)(2,1)} %bitcast.13, s32[1024]{0:T(1024)S(1)} %pad_clamp_fusion), kind=kCustom, calls=%fused_computation.1 | custom fusion | bytes 8388864 | tf_op jit(solution)/shard_map/gather | solution.py:588
  8.0 0.0 copy-done.3
  8.0 3.9 %fusion.5 = (bf16[16,16,2048]{2,1,0:T(8,128)(2,1)S(1)}, bf16[16,16,2048]{2,1,0:T(8,128)(2,1)}, bf16[16,16,2048]{2,1,0:T(8,128)(2,1)}, bf16[16,16,2048]{2,1,0:T(8,128)(2,1)S(1)}) fusion(bf16[64,16,2048]{2,1,0:T(8,128)(2,1)} %gather_fusion.1), kind=kLoop, calls=%fused_computation.31 | loop fusion | bytes 8388608 | tf_op jit(solution)/shard_map/slice | solution.py:590
  11.9 1.4 collective-permute-start.1
  13.3 0.0 collective-permute-start
  13.3 1.7 collective-permute-start.2
  15.1 52.7 %shard_map.64.first_ref = s16[2,4,528,512]{3,2,1,0:T(8,128)(2,1)} custom-call(bf16[512,2048]{1,0:T(8,128)(2,1)} %hidden_ref.3, bf16[2048,8192]{1,0:T(8,128)(2,1)} %weight_ref.3), custom_call_target="tpu_custom_call" | custom-call | flops 44999999488 | bytes 45000000 | tf_op jit(solution)/shard_map/pallas_call | solution.py:417
  67.8 0.1 min.12.held_ref
  67.9 0.0 collective-permute-done.5
  67.9 0.0 collective-permute-start.3
  67.9 0.0 collective-permute-done.4
  67.9 3.0 %collective-permute-done.3 = s32[16]{0:T(128)S(1)} collective-permute-done((s32[16]{0:T(128)S(1)}, s32[16]{0:T(128)S(1)}, u32[]{:S(2)}, u32[]{:S(2)}) %collective-permute-start.3) | collective-permute-done | bytes 96 | tf_op jit(solution)/shard_map/ppermute | solution.py:560
  70.9 0.1 pad_add_fusion.slots_ref
  70.9 0.0 collective-permute-done.1
  71.0 0.0 collective-permute-done
  71.0 0.0 collective-permute-done.2
  71.0 1.8 pad_maximum_fusion.rows_ref
  72.8 11.1 %shard_map.65.in_ref = f32[32,16,128]{2,1,0:T(8,128)S(1)} custom-call(s32[64]{0:T(128)S(1)} %pad_add_fusion.slots_ref, bf16[64,16,2048]{2,1,0:T(8,128)(2,1)S(1)} %pad_maximum_fusion.rows_ref, bf16[64,64,2048]{2,1,0:T(8,128)(2,1)} %refs_7_.2, bf16[64,64,2048]{2,1,0:T(8,128)(2,1)} %refs_7_.2, bf16[64,64,2048]{2,1,0:T(8,128)(2,1)} %refs_7_.2, ...), custom_call_target="tpu_custom_call" | custom-call | tf_op jit(solution)/shard_map/pallas_call | solution.py:57
  83.9 14.2 %shard_map.66.rank_ref = f32[32,16,128]{2,1,0:T(8,128)S(1)} custom-call(f32[32,16,128]{2,1,0:T(8,128)S(1)} %shard_map.65.in_ref), custom_call_target="tpu_custom_call" | custom-call | tf_op jit(solution)/shard_map/pallas_call | solution.py:509
  98.1 9.8 %shard_map.67 = f32[64,16,2048]{2,1,0:T(8,128)S(1)} custom-call(s32[64]{0:T(128)S(1)} %pad_add_fusion.slots_ref, f32[32,16,128]{2,1,0:T(8,128)S(1)} %shard_map.66.rank_ref, bf16[64,64,2048]{2,1,0:T(8,128)(2,1)} %refs_7_.3, bf16[64,64,2048]{2,1,0:T(8,128)(2,1)} %refs_7_.3, bf16[64,64,2048]{2,1,0:T(8,128)(2,1)} %refs_7_.3, bf16[64,64,2048]{2,1,0:T(8,128)(2,1)} %refs_7_.3, ...), custom_call_target="tpu_custom_call" | custom-call | tf_op jit(solution)/shard_map/pallas_call | solution.py:57
  107.9 2.8 %fusion.4 = (f32[16,16,2048]{2,1,0:T(8,128)}, f32[16,16,2048]{2,1,0:T(8,128)}, f32[16,16,2048]{2,1,0:T(8,128)}, f32[16,16,2048]{2,1,0:T(8,128)S(1)}) fusion(f32[64,16,2048]{2,1,0:T(8,128)S(1)} %shard_map.67), kind=kLoop, calls=%fused_computation.30 | loop fusion | bytes 16777216 | tf_op jit(solution)/shard_map/slice | solution.py:600
  110.8 0.0 collective-permute-start.8
  110.8 1.5 collective-permute-start.7
  112.3 0.0 copy-start.4
  112.3 1.4 collective-permute-start.6
  113.7 104.0 %shard_map.68.base_ref = f32[4,512,512]{2,1,0:T(8,128)} custom-call(bf16[512,2048]{1,0:T(8,128)(2,1)} %hidden_ref.3, bf16[2048,8192]{1,0:T(8,128)(2,1)} %weight_ref.3, s16[2,4,528,512]{3,2,1,0:T(8,128)(2,1)} %shard_map.64.first_ref), custom_call_target="tpu_custom_call" | custom-call | flops 89999998976 | bytes 90000000 | tf_op jit(solution)/shard_map/pallas_call | solution.py:434
  217.8 0.0 collective-permute-done.8.refs_3_
  217.8 0.0 collective-permute-done.7.refs_2_
  217.8 0.0 collective-permute-done.6.refs_1_
  217.8 0.0 copy-start.1
  217.8 0.0 copy-done.4
  217.8 0.0 copy-start.2
  217.9 2.2 copy-done.2
  220.0 17.6 %shard_map.69 = bf16[512,2048]{1,0:T(8,128)(2,1)} custom-call(s32[128]{0:T(128)S(1)} %min.12.held_ref, s32[32]{0:T(128)S(1)} %copy-done.4, f32[4,512,512]{2,1,0:T(8,128)S(1)} %copy-done.2, f32[16,16,2048]{2,1,0:T(8,128)S(1)} %get-tuple-element.18.refs_0_, f32[16,16,2048]{2,1,0:T(8,128)} %collective-permute-done.6.refs_1_, ...), custom_call_target="tpu_custom_call" | custom-call | tf_op jit(solution)/shard_map/pallas_call | solution.py:545
  237.6 0.0 copy-done.1
  (8 shorter events, 0.1 us)
Async XLA Ops:
  0.0 0.7 copy-start
  1.4 6.6 %copy-start.3 = (s32[32]{0:T(128)}, s32[32]{0:T(128)S(1)}, u32[]{:S(2)}) copy-start(s32[32]{0:T(128)S(1)} %get-tuple-element.32.rel_ref) | copy-start | bytes 388
  1.9 66.0 %collective-permute-start.5 = (s32[16]{0:T(128)S(1)}, s32[16]{0:T(128)S(1)}, u32[]{:S(2)}, u32[]{:S(2)}) collective-permute-start(s32[16]{0:T(128)S(1)} %get-tuple-element.24), channel_id=1, source_target_pairs={{0,3},{1,0},{2,1},{3,2},{4,7},{5,4},{6,5},{7,6},{8,11},{9,8},{10,9... | collective-permute-start | bytes 200 | tf_op jit(solution)/shard_map/ppermute | solution.py:560
  2.9 65.0 %collective-permute-start.4 = (s32[16]{0:T(128)S(1)}, s32[16]{0:T(128)S(1)}, u32[]{:S(2)}, u32[]{:S(2)}) collective-permute-start(s32[16]{0:T(128)S(1)} %get-tuple-element.25), channel_id=1, source_target_pairs={{0,2},{1,3},{2,0},{3,1},{4,6},{5,7},{6,4},{7,5},{8,10},{9,11},{10,... | collective-permute-start | bytes 200 | tf_op jit(solution)/shard_map/ppermute | solution.py:560
  11.9 59.0 %collective-permute-start.1 = (bf16[16,16,2048]{2,1,0:T(8,128)(2,1)}, bf16[16,16,2048]{2,1,0:T(8,128)(2,1)S(1)}, u32[]{:S(2)}, u32[]{:S(2)}) collective-permute-start(bf16[16,16,2048]{2,1,0:T(8,128)(2,1)} %get-tuple-element.20), channel_id=1, source_target_pairs={{0,2},{1,3},{2,0},{3,1},{4,6},{5,7},{6,4},{7,5},{8,10},{9,11},{10,... | collective-permute-start | bytes 3145736 | tf_op jit(solution)/shard_map/ppermute | solution.py:560
  13.3 57.6 %collective-permute-start = (bf16[16,16,2048]{2,1,0:T(8,128)(2,1)}, bf16[16,16,2048]{2,1,0:T(8,128)(2,1)}, u32[]{:S(2)}, u32[]{:S(2)}) collective-permute-start(bf16[16,16,2048]{2,1,0:T(8,128)(2,1)} %get-tuple-element.21), channel_id=1, source_target_pairs={{0,1},{1,2},{2,3},{3,0},{4,5},{5,6},{6,7},{7,4},{8,9},{9,10},{10,1... | collective-permute-start | bytes 3145736 | tf_op jit(solution)/shard_map/ppermute | solution.py:560
  13.3 57.6 %collective-permute-start.2 = (bf16[16,16,2048]{2,1,0:T(8,128)(2,1)S(1)}, bf16[16,16,2048]{2,1,0:T(8,128)(2,1)}, u32[]{:S(2)}, u32[]{:S(2)}) collective-permute-start(bf16[16,16,2048]{2,1,0:T(8,128)(2,1)S(1)} %get-tuple-element.22), channel_id=1, source_target_pairs={{0,3},{1,0},{2,1},{3,2},{4,7},{5,4},{6,5},{7,6},{8,11},{9,8},{10,9... | collective-permute-start | bytes 3145736 | tf_op jit(solution)/shard_map/ppermute | solution.py:560
  67.9 3.0 %collective-permute-start.3 = (s32[16]{0:T(128)S(1)}, s32[16]{0:T(128)S(1)}, u32[]{:S(2)}, u32[]{:S(2)}) collective-permute-start(s32[16]{0:T(128)S(1)} %get-tuple-element.26), channel_id=1, source_target_pairs={{0,1},{1,2},{2,3},{3,0},{4,5},{5,6},{6,7},{7,4},{8,9},{9,10},{10,1... | collective-permute-start | bytes 200 | tf_op jit(solution)/shard_map/ppermute | solution.py:560
  110.8 107.0 %collective-permute-start.8 = (f32[16,16,2048]{2,1,0:T(8,128)}, f32[16,16,2048]{2,1,0:T(8,128)S(1)}, u32[]{:S(2)}, u32[]{:S(2)}) collective-permute-start(f32[16,16,2048]{2,1,0:T(8,128)} %get-tuple-element.15), channel_id=1, source_target_pairs={{0,1},{1,2},{2,3},{3,0},{4,5},{5,6},{6,7},{7,4},{8,9},{9,10},{10,1... | collective-permute-start | bytes 6291464 | tf_op jit(solution)/shard_map/ppermute | solution.py:560
  110.8 107.0 %collective-permute-start.7 = (f32[16,16,2048]{2,1,0:T(8,128)}, f32[16,16,2048]{2,1,0:T(8,128)}, u32[]{:S(2)}, u32[]{:S(2)}) collective-permute-start(f32[16,16,2048]{2,1,0:T(8,128)} %get-tuple-element.16), channel_id=1, source_target_pairs={{0,2},{1,3},{2,0},{3,1},{4,6},{5,7},{6,4},{7,5},{8,10},{9,11},{10,... | collective-permute-start | bytes 6291464 | tf_op jit(solution)/shard_map/ppermute | solution.py:560
  112.3 105.5 %copy-start.4 = (s32[32]{0:T(128)S(1)}, s32[32]{0:T(128)}, u32[]{:S(2)}) copy-start(s32[32]{0:T(128)} %copy-done.3) | copy-start | bytes 388
  112.3 105.5 %collective-permute-start.6 = (f32[16,16,2048]{2,1,0:T(8,128)}, f32[16,16,2048]{2,1,0:T(8,128)}, u32[]{:S(2)}, u32[]{:S(2)}) collective-permute-start(f32[16,16,2048]{2,1,0:T(8,128)} %get-tuple-element.17), channel_id=1, source_target_pairs={{0,3},{1,0},{2,1},{3,2},{4,7},{5,4},{6,5},{7,6},{8,11},{9,8},{10,9... | collective-permute-start | bytes 6291464 | tf_op jit(solution)/shard_map/ppermute | solution.py:560
  217.8 19.8 %copy-start.1 = (s32[256]{0:T(256)S(1)}, s32[256]{0:T(256)}, u32[]{:S(2)}) copy-start(s32[256]{0:T(256)} %param.10) | copy-start | bytes 3076
  217.8 2.2 copy-start.2

commit v3 on v2

--- a/solution.py
+++ b/solution.py
@@ -9,6 +9,7 @@
 
 MIB = 1024 * 1024
 STEP = 8
+PAIR = 2
 
 
 def down_kernel(step, slots_ref, rows_ref, *refs):
@@ -526,12 +527,17 @@
 def join_kernel(held_ref, rel_ref, base_ref, *refs):
     deltas, out_ref = refs[:-1], refs[-1]
     pieces, _, cols = base_ref.shape
-    for k, delta in enumerate(deltas):
-        @pl.when(rel_ref[pl.program_id(0)] == k)
-        def _():
-            for c in range(pieces):
-                part = slice(c * cols, (c + 1) * cols)
-                out_ref[:, part] = (base_ref[c] + delta[0, :, part]).astype(out_ref.dtype)
+    block = deltas[0].shape[1]
+    for i in range(PAIR):
+        span = slice(i * block, (i + 1) * block)
+        for k, delta in enumerate(deltas[i::PAIR]):
+            @pl.when(rel_ref[pl.program_id(0) * PAIR + i] == k)
+            def _():
+                for c in range(pieces):
+                    part = slice(c * cols, (c + 1) * cols)
+                    out_ref[span, part] = (base_ref[c, span] + delta[0, :, part]).astype(
+                        out_ref.dtype
+                    )
 
 
 def join(base, deltas, held, rel):
@@ -539,21 +545,23 @@
     segs = rel.shape[0]
     _, block, width = deltas[0].shape
 
-    def spec(k):
-        return pl.BlockSpec((1, block, width), lambda s, held, rel: (held[k * segs + s], 0, 0))
+    def spec(k, i):
+        return pl.BlockSpec(
+            (1, block, width), lambda s, held, rel: (held[k * segs + s * PAIR + i], 0, 0)
+        )
 
     return pl.pallas_call(
         join_kernel,
         grid_spec=pltpu.PrefetchScalarGridSpec(
             num_scalar_prefetch=2,
-            grid=(segs,),
-            in_specs=[pl.BlockSpec((pieces, block, cols), lambda s, held, rel: (0, s, 0))]
-            + [spec(k) for k in range(len(deltas))],
-            out_specs=pl.BlockSpec((block, width), lambda s, held, rel: (s, 0)),
+            grid=(segs // PAIR,),
+            in_specs=[pl.BlockSpec((pieces, PAIR * block, cols), lambda s, held, rel: (0, s, 0))]
+            + [spec(k, i) for k in range(len(deltas)) for i in range(PAIR)],
+            out_specs=pl.BlockSpec((PAIR * block, width), lambda s, held, rel: (s, 0)),
         ),
         out_shape=jax.ShapeDtypeStruct((rows, width), jnp.bfloat16),
         compiler_params=pltpu.CompilerParams(vmem_limit_bytes=16 * MIB),
-    )(held, rel, base, *deltas)
+    )(held, rel, base, *[d for d in deltas for _ in range(PAIR)])
 
 
 def shift(x, by, count):
@@ -585,9 +593,10 @@
     wanted = jnp.sum(jnp.where(match, local[None, None, :], 0), axis=2)
     held = jnp.clip(running, 0, cap - 1).astype(jnp.int32).reshape(-1)
     seg_rows = hidden.reshape(segs, block, width)
-    out_rows = seg_rows[picked]
     got_slots = [wanted[0]] + [shift(wanted[k], k, dp) for k in range(1, dp)]
-    got_rows = [out_rows[0]] + [shift(out_rows[k], k, dp) for k in range(1, dp)]
+    got_rows = [seg_rows[picked[0]]] + [
+        shift(seg_rows[picked[k]], k, dp) for k in range(1, dp)
+    ]
     slots = jnp.concatenate(got_slots)
     there_rows = jnp.concatenate(got_rows)
     first, rest = base_parts(hidden, output_weight)

time: 241 us -> 233 us (0.967); the launches traced: 238 us -> 232 us
  Pallas kernels: 210 us -> 204 us
    pallas_call x1, Pallas kernels: 17.6 us -> 11.3 us  [join(): pl.pallas_call(join_kernel, grid_spec=pltpu.PrefetchScalarGridSpec(num_sc...]
    slice x1 -> x0, local copies, waits for them, and re-layouts: 3.94 us -> none  [per_device(): got_rows = [out_rows[0]] + [shift(out_rows[k], k, dp) for k in range(1, dp)]]
    gather x1 -> x4, local copies, waits for them, and re-layouts: 4.35 us -> 7.12 us  [the longest x3 6.5 us: per_device(): seg_rows[picked[k]]]
  transfers between devices with their start and end apart: 9 -> 9, of which waited for: 1 -> 1; matrix products, arithmetic and copies ran while one was open for 4% -> 3% of each run, Pallas kernels for 66% -> 68%
where the time goes in v3:
time: 233 us; the launch traced here: 232 us
  Pallas kernels  204 us (88%)
  local copies, waits for them, and re-layouts  12.9 us (6%)
  starting transfers between devices  8.62 us (4%)
  other arithmetic  3.54 us (2%)
  waiting for transfers between devices  2.96 us (1%)
    pallas_call x1, Pallas kernels, rest(): pl.pallas_call(functools.partial(rest_kernel, 'tensor', count, pieces), o...  104 us
    pallas_call x1, Pallas kernels, first(): pl.pallas_call(functools.partial(first_kernel, 'tensor', count, pieces),...  54.3 us
    pallas_call x2, Pallas kernels, apply_maps(): pl.pallas_call(functools.partial(kernel, step), grid_spec=pltpu.PrefetchS...  20 us
    pallas_call x1, Pallas kernels, sum_over_tensor(): pl.pallas_call(functools.partial(sum_kernel, 'tensor', count), out_shape=...  14.6 us
    pallas_call x1, Pallas kernels, join(): pl.pallas_call(join_kernel, grid_spec=pltpu.PrefetchScalarGridSpec(num_sc...  11.3 us
    ppermute x9, starting transfers between devices, shift(): return lax.ppermute(x, 'dp', [(i, (i + by) % count) for i in range(count)])  8.62 us
    gather x3, local copies, waits for them, and re-layouts, per_device(): seg_rows[picked[k]]  6.5 us
  transfers between devices with their start and end apart: 9, of which 1 were waited for; matrix products, arithmetic and copies ran while one was open for 3% of the time, Pallas kernels for 68%

profile of v3, /device:TPU:16, one launch (start us, length us, event | category | flops | bytes accessed | tf_op | source)
XLA Modules:
  0.0 232.3 jit_solution(13748774390703786126)
XLA Ops:
  0.0 0.0 copy-start
  0.0 0.0 copy-start.5
  0.0 0.8 compare_select_fusion.4
  0.8 0.0 copy-done
  0.8 0.7 gather_fusion
  1.6 0.0 copy-start.3
  1.6 0.2 reduce_window_sum.11
  1.8 0.2 fusion.1
  2.1 1.0 collective-permute-start.5
  3.0 0.6 collective-permute-start.4
  3.7 3.2 %gather_fusion.4 = bf16[16,16,2048]{2,1,0:T(8,128)(2,1)} fusion(bf16[32,16,2048]{2,1,0:T(8,128)(2,1)} %bitcast.25, s32[1024]{0:T(1024)S(1)} %pad_clamp_fusion), kind=kCustom, calls=%fused_computation.4 | custom fusion | bytes 2097216 | tf_op jit(solution)/shard_map/gather | solution.py:598
  6.9 0.3 collective-permute-start.2
  7.2 0.0 copy-done.5
  7.2 1.7 gather_fusion.3
  8.8 0.0 copy-done.3
  8.8 1.5 collective-permute-start.1
  10.4 1.7 gather_fusion.2
  12.0 0.0 copy-start.6
  12.0 0.0 collective-permute-start
  12.0 54.3 %shard_map.64.first_ref = s16[2,4,528,512]{3,2,1,0:T(8,128)(2,1)} custom-call(bf16[512,2048]{1,0:T(8,128)(2,1)} %hidden_ref.3, bf16[2048,8192]{1,0:T(8,128)(2,1)} %weight_ref.3), custom_call_target="tpu_custom_call" | custom-call | flops 44999999488 | bytes 45000000 | tf_op jit(solution)/shard_map/pallas_call | solution.py:418
  66.4 0.1 min.12.held_ref
  66.5 0.0 copy-done.6
  66.5 0.6 gather_fusion.1
  67.1 0.0 collective-permute-done.5
  67.1 0.1 collective-permute-start.3
  67.2 0.0 collective-permute-done.4
  67.2 2.9 %collective-permute-done.3 = s32[16]{0:T(128)S(1)} collective-permute-done((s32[16]{0:T(128)S(1)}, s32[16]{0:T(128)S(1)}, u32[]{:S(2)}, u32[]{:S(2)}) %collective-permute-start.3) | collective-permute-done | bytes 96 | tf_op jit(solution)/shard_map/ppermute | solution.py:568
  70.1 0.1 pad_add_fusion.slots_ref
  70.2 0.0 collective-permute-done.2
  70.2 0.0 collective-permute-done.1
  70.2 0.0 collective-permute-done
  70.2 2.1 pad_maximum_fusion.rows_ref
  72.3 10.4 %shard_map.65.in_ref = f32[32,16,128]{2,1,0:T(8,128)S(1)} custom-call(s32[64]{0:T(128)S(1)} %pad_add_fusion.slots_ref, bf16[64,16,2048]{2,1,0:T(8,128)(2,1)S(1)} %pad_maximum_fusion.rows_ref, bf16[64,64,2048]{2,1,0:T(8,128)(2,1)} %refs_7_.2, bf16[64,64,2048]{2,1,0:T(8,128)(2,1)} %refs_7_.2, bf16[64,64,2048]{2,1,0:T(8,128)(2,1)} %refs_7_.2, ...), custom_call_target="tpu_custom_call" | custom-call | tf_op jit(solution)/shard_map/pallas_call | solution.py:58
  82.8 14.6 %shard_map.66.rank_ref = f32[32,16,128]{2,1,0:T(8,128)S(1)} custom-call(f32[32,16,128]{2,1,0:T(8,128)S(1)} %shard_map.65.in_ref), custom_call_target="tpu_custom_call" | custom-call | tf_op jit(solution)/shard_map/pallas_call | solution.py:510
  97.4 9.6 %shard_map.67 = f32[64,16,2048]{2,1,0:T(8,128)S(1)} custom-call(s32[64]{0:T(128)S(1)} %pad_add_fusion.slots_ref, f32[32,16,128]{2,1,0:T(8,128)S(1)} %shard_map.66.rank_ref, bf16[64,64,2048]{2,1,0:T(8,128)(2,1)} %refs_7_.3, bf16[64,64,2048]{2,1,0:T(8,128)(2,1)} %refs_7_.3, bf16[64,64,2048]{2,1,0:T(8,128)(2,1)} %refs_7_.3, bf16[64,64,2048]{2,1,0:T(8,128)(2,1)} %refs_7_.3, ...), custom_call_target="tpu_custom_call" | custom-call | tf_op jit(solution)/shard_map/pallas_call | solution.py:58
  107.0 2.8 %fusion.8 = (f32[16,16,2048]{2,1,0:T(8,128)}, f32[16,16,2048]{2,1,0:T(8,128)}, f32[16,16,2048]{2,1,0:T(8,128)}, f32[16,16,2048]{2,1,0:T(8,128)S(1)}) fusion(f32[64,16,2048]{2,1,0:T(8,128)S(1)} %shard_map.67), kind=kLoop, calls=%fused_computation.43 | loop fusion | bytes 16777216 | tf_op jit(solution)/shard_map/slice | solution.py:609
  109.8 0.0 collective-permute-start.8
  109.8 3.7 %collective-permute-start.7 = (f32[16,16,2048]{2,1,0:T(8,128)}, f32[16,16,2048]{2,1,0:T(8,128)}, u32[]{:S(2)}, u32[]{:S(2)}) collective-permute-start(f32[16,16,2048]{2,1,0:T(8,128)} %get-tuple-element.16), channel_id=1, source_target_pairs={{0,2},{1,3},{2,0},{3,1},{4,6},{5,7},{6,4},{7,5},{8,10},{9,11},{10,... | collective-permute-start | bytes 6291464 | tf_op jit(solution)/shard_map/ppermute | solution.py:568
  113.5 1.4 collective-permute-start.6
  114.9 103.8 %shard_map.68.base_ref = f32[4,512,512]{2,1,0:T(8,128)} custom-call(bf16[512,2048]{1,0:T(8,128)(2,1)} %hidden_ref.3, bf16[2048,8192]{1,0:T(8,128)(2,1)} %weight_ref.3, s16[2,4,528,512]{3,2,1,0:T(8,128)(2,1)} %shard_map.64.first_ref), custom_call_target="tpu_custom_call" | custom-call | flops 89999998976 | bytes 90000000 | tf_op jit(solution)/shard_map/pallas_call | solution.py:435
  218.7 0.0 collective-permute-done.8.refs_6_.refs_7_
  218.7 0.0 collective-permute-done.7.refs_4_.refs_5_
  218.7 0.0 collective-permute-done.6.refs_2_.refs_3_
  218.7 0.0 copy-done.4
  218.8 0.0 copy-start.2
  218.8 2.2 copy-done.2
  220.9 11.3 %shard_map.69 = bf16[512,2048]{1,0:T(8,128)(2,1)} custom-call(s32[128]{0:T(128)S(1)} %min.12.held_ref, s32[32]{0:T(128)S(1)} %copy-done.4, f32[4,512,512]{2,1,0:T(8,128)S(1)} %copy-done.2, f32[16,16,2048]{2,1,0:T(8,128)S(1)} %get-tuple-element.18.refs_0_.refs_1_, f32[16,16,2048]{2,1,0:T(8,128)S(1)} %get-tuple-element.18.refs_0_.refs_1_, ...), custom_call_target="tpu_custom_call" | custom-call | tf_op jit(solution)/shard_map/pallas_call | solution.py:553
  232.3 0.0 copy-done.1
  (13 shorter events, 0.1 us)
Async XLA Ops:
  0.0 0.8 copy-start
  0.0 7.2 %copy-start.5 = (bf16[512,2048]{1,0:T(8,128)(2,1)S(1)}, bf16[512,2048]{1,0:T(8,128)(2,1)}, u32[]{:S(2)}) copy-start(bf16[512,2048]{1,0:T(8,128)(2,1)} %hidden_ref.3) | copy-start | bytes 6291460
  1.6 7.3 %copy-start.3 = (s32[32]{0:T(128)}, s32[32]{0:T(128)S(1)}, u32[]{:S(2)}) copy-start(s32[32]{0:T(128)S(1)} %get-tuple-element.32.rel_ref) | copy-start | bytes 388
  2.1 65.0 %collective-permute-start.5 = (s32[16]{0:T(128)S(1)}, s32[16]{0:T(128)S(1)}, u32[]{:S(2)}, u32[]{:S(2)}) collective-permute-start(s32[16]{0:T(128)S(1)} %get-tuple-element.20), channel_id=1, source_target_pairs={{0,3},{1,0},{2,1},{3,2},{4,7},{5,4},{6,5},{7,6},{8,11},{9,8},{10,9... | collective-permute-start | bytes 200 | tf_op jit(solution)/shard_map/ppermute | solution.py:568
  3.0 64.1 %collective-permute-start.4 = (s32[16]{0:T(128)S(1)}, s32[16]{0:T(128)S(1)}, u32[]{:S(2)}, u32[]{:S(2)}) collective-permute-start(s32[16]{0:T(128)S(1)} %get-tuple-element.21), channel_id=1, source_target_pairs={{0,2},{1,3},{2,0},{3,1},{4,6},{5,7},{6,4},{7,5},{8,10},{9,11},{10,... | collective-permute-start | bytes 200 | tf_op jit(solution)/shard_map/ppermute | solution.py:568
  6.9 63.3 %collective-permute-start.2 = (bf16[16,16,2048]{2,1,0:T(8,128)(2,1)}, bf16[16,16,2048]{2,1,0:T(8,128)(2,1)}, u32[]{:S(2)}, u32[]{:S(2)}) collective-permute-start(bf16[16,16,2048]{2,1,0:T(8,128)(2,1)} %gather_fusion.4), channel_id=1, source_target_pairs={{0,3},{1,0},{2,1},{3,2},{4,7},{5,4},{6,5},{7,6},{8,11},{9,8},{10,9... | collective-permute-start | bytes 3145736 | tf_op jit(solution)/shard_map/ppermute | solution.py:568
  8.8 61.4 %collective-permute-start.1 = (bf16[16,16,2048]{2,1,0:T(8,128)(2,1)}, bf16[16,16,2048]{2,1,0:T(8,128)(2,1)}, u32[]{:S(2)}, u32[]{:S(2)}) collective-permute-start(bf16[16,16,2048]{2,1,0:T(8,128)(2,1)} %gather_fusion.3), channel_id=1, source_target_pairs={{0,2},{1,3},{2,0},{3,1},{4,6},{5,7},{6,4},{7,5},{8,10},{9,11},{10,... | collective-permute-start | bytes 3145736 | tf_op jit(solution)/shard_map/ppermute | solution.py:568
  12.0 54.4 %copy-start.6 = (bf16[512,2048]{1,0:T(8,128)(2,1)S(1)}, bf16[512,2048]{1,0:T(8,128)(2,1)}, u32[]{:S(2)}) copy-start(bf16[512,2048]{1,0:T(8,128)(2,1)} %hidden_ref.3) | copy-start | bytes 6291460
  12.0 58.2 %collective-permute-start = (bf16[16,16,2048]{2,1,0:T(8,128)(2,1)}, bf16[16,16,2048]{2,1,0:T(8,128)(2,1)}, u32[]{:S(2)}, u32[]{:S(2)}) collective-permute-start(bf16[16,16,2048]{2,1,0:T(8,128)(2,1)} %gather_fusion.2), channel_id=1, source_target_pairs={{0,1},{1,2},{2,3},{3,0},{4,5},{5,6},{6,7},{7,4},{8,9},{9,10},{10,1... | collective-permute-start | bytes 3145736 | tf_op jit(solution)/shard_map/ppermute | solution.py:568
  67.1 3.0 %collective-permute-start.3 = (s32[16]{0:T(128)S(1)}, s32[16]{0:T(128)S(1)}, u32[]{:S(2)}, u32[]{:S(2)}) collective-permute-start(s32[16]{0:T(128)S(1)} %get-tuple-element.22), channel_id=1, source_target_pairs={{0,1},{1,2},{2,3},{3,0},{4,5},{5,6},{6,7},{7,4},{8,9},{9,10},{10,1... | collective-permute-start | bytes 200 | tf_op jit(solution)/shard_map/ppermute | solution.py:568
  109.8 108.9 %collective-permute-start.8 = (f32[16,16,2048]{2,1,0:T(8,128)}, f32[16,16,2048]{2,1,0:T(8,128)S(1)}, u32[]{:S(2)}, u32[]{:S(2)}) collective-permute-start(f32[16,16,2048]{2,1,0:T(8,128)} %get-tuple-element.15), channel_id=1, source_target_pairs={{0,1},{1,2},{2,3},{3,0},{4,5},{5,6},{6,7},{7,4},{8,9},{9,10},{10,1... | collective-permute-start | bytes 6291464 | tf_op jit(solution)/shard_map/ppermute | solution.py:568
  109.8 108.9 %collective-permute-start.7 = (f32[16,16,2048]{2,1,0:T(8,128)}, f32[16,16,2048]{2,1,0:T(8,128)}, u32[]{:S(2)}, u32[]{:S(2)}) collective-permute-start(f32[16,16,2048]{2,1,0:T(8,128)} %get-tuple-element.16), channel_id=1, source_target_pairs={{0,2},{1,3},{2,0},{3,1},{4,6},{5,7},{6,4},{7,5},{8,10},{9,11},{10,... | collective-permute-start | bytes 6291464 | tf_op jit(solution)/shard_map/ppermute | solution.py:568
  113.5 105.3 %copy-start.4 = (s32[32]{0:T(128)S(1)}, s32[32]{0:T(128)}, u32[]{:S(2)}) copy-start(s32[32]{0:T(128)} %copy-done.3) | copy-start | bytes 388
  113.5 105.3 %collective-permute-start.6 = (f32[16,16,2048]{2,1,0:T(8,128)}, f32[16,16,2048]{2,1,0:T(8,128)}, u32[]{:S(2)}, u32[]{:S(2)}) collective-permute-start(f32[16,16,2048]{2,1,0:T(8,128)} %get-tuple-element.17), channel_id=1, source_target_pairs={{0,3},{1,0},{2,1},{3,2},{4,7},{5,4},{6,5},{7,6},{8,11},{9,8},{10,9... | collective-permute-start | bytes 6291464 | tf_op jit(solution)/shard_map/ppermute | solution.py:568
  218.8 2.2 copy-start.2
  220.9 11.3 %copy-start.1 = (s32[256]{0:T(256)S(1)}, s32[256]{0:T(256)}, u32[]{:S(2)}) copy-start(s32[256]{0:T(256)} %param.10) | copy-start | bytes 3076
